TPU v7x, 32 devices: a whole 2x2x4 slice. The times are simulated.
32 devices in a mesh: role: 4 (over y, core), rep: 2 (over x), tp: 4 (over z).
Axes of the slice: x: 2, y: 2, z: 4, core: 2. Of those that a mesh axis runs over, the one named last changes fastest.
Arguments:
- span_hidden: bfloat16 [4096, 8192], P(('role', 'rep'), 'tp'), may hold values from -6 to 6
- key_value_weight: bfloat16 [8192, 2048], P('tp'), may hold values from -0.0625 to 0.0625
- queries: bfloat16 [128, 8192], P(('role', 'rep'), 'tp'), may hold values from -200 to 200
- kv_cache: bfloat16 [36864, 2048], P(('role', 'rep'), 'tp'), may hold values from -6 to 6, as said below
- block_table: int32 [128, 4], P(('role', 'rep')), may hold values from 0 to 35, as said below
- lengths: int32 [128], P(('role', 'rep')), may hold values from 1 to 512, as said below
- placement: int32 [8], replicated, may hold values from 0 to 127
Outputs:
- attention_out: bfloat16 [128, 8192], P(('role', 'rep'), 'tp')
Inputs may be any that keep to these rules, and one draw needn't show every extreme that they name: `lengths`: one request of every replica has exactly 512 cached tokens. `block_table`: the first ceil(lengths / 128) entries of a request's row are distinct pages used by no other request of its replica; later entries are arbitrary pages of the pool. `kv_cache`: the 1 column blocks that hold the same KV head are equal.
All inputs are finite; a program needn't handle non-finite values.
Results may differ from a plain program's by a relative error of at most 0.0045.
Values may be sent and summed in bfloat16 or wider, within the bound.
A program may use at most 128 MiB of HBM per device.

v0:
```python
import jax
import jax.numpy as jnp
from jax import lax
from jax.sharding import PartitionSpec as P

HEAD_SIZE = 128
PAGE_TOKENS = 128


masked_score = -1e30


def cache_visibility(pages_table, cache_lengths, pool_pages):
    page_slots = pages_table.shape[1]
    matched = pages_table[:, :, None] == jnp.arange(pool_pages, dtype=jnp.int32)[None, None, :]
    position = (
        jnp.arange(page_slots, dtype=jnp.int32)[:, None] * PAGE_TOKENS
        + jnp.arange(PAGE_TOKENS, dtype=jnp.int32)[None, :]
    )
    inside = position[None, :, :] < cache_lengths[:, None, None]
    visible = jnp.any(matched[:, :, :, None] & inside[:, :, None, :], axis=1)
    return visible.reshape(pages_table.shape[0], pool_pages * PAGE_TOKENS)


def partial_state(query_heads, kv_rows, visible):
    scores = jnp.einsum(
        "rhgd,nhd->rhgn", query_heads, kv_rows[:, :, 0], preferred_element_type=jnp.float32
    ) * HEAD_SIZE ** (-0.5)
    seen = visible[:, None, None, :]
    scores = jnp.where(seen, scores, masked_score)
    row_max = jnp.max(scores, axis=-1)
    probs = jnp.where(seen, jnp.exp(scores - row_max[..., None]), 0.0)
    totals = jnp.sum(probs, axis=-1)
    weighted = jnp.einsum(
        "rhgn,nhd->rhgd",
        probs.astype(jnp.bfloat16),
        kv_rows[:, :, 1],
        preferred_element_type=jnp.float32,
    )
    return (row_max, totals, weighted)


def combine_states(first, second):
    joint = jnp.maximum(first[0], second[0])
    left = jnp.exp(first[0] - joint)
    right = jnp.exp(second[0] - joint)
    totals = first[1] * left + second[1] * right
    weighted = first[2] * left[..., None] + second[2] * right[..., None]
    return (joint, totals, weighted)


def local(span_hidden, key_value_weight, queries, kv_cache, block_table, lengths, placement):
    span_rows = span_hidden.shape[0]
    full_width = key_value_weight.shape[1]
    tp_count = lax.axis_size("tp")
    rows_local = span_rows // tp_count
    local_width = kv_cache.shape[1]
    groups = full_width // local_width
    copies = tp_count // groups
    fresh_tokens = lax.psum_scatter(
        jnp.dot(span_hidden, key_value_weight, preferred_element_type=jnp.float32),
        "tp",
        scatter_dimension=0,
        tiled=True,
    ).astype(jnp.bfloat16)
    outgoing = fresh_tokens.reshape(rows_local, groups, 1, local_width)
    outgoing = jnp.broadcast_to(outgoing, (rows_local, groups, copies, local_width)).reshape(
        rows_local, tp_count, local_width
    )
    arrived = lax.all_to_all(outgoing, "tp", split_axis=1, concat_axis=0, tiled=True).reshape(
        span_rows, local_width
    )
    kv_local = local_width // (2 * HEAD_SIZE)
    request_count = queries.shape[0]
    qd_width = queries.shape[1]
    group_size = qd_width // HEAD_SIZE // kv_local
    query_heads = queries.reshape(request_count, kv_local, group_size, HEAD_SIZE)
    replica = lax.axis_index(("role", "rep"))
    request_ids = replica * request_count + jnp.arange(request_count, dtype=jnp.int32)
    pool_rows = kv_cache.shape[0]
    seen_cache = cache_visibility(block_table, lengths, pool_rows // PAGE_TOKENS)
    cache_state = partial_state(
        query_heads, kv_cache.reshape(pool_rows, kv_local, 2, HEAD_SIZE), seen_cache
    )
    owner_rows = jnp.repeat(placement, span_rows)
    shape_state = (request_count, kv_local, group_size)
    initial = (
        jnp.full(shape_state, masked_score, jnp.float32),
        jnp.zeros(shape_state, jnp.float32),
        jnp.zeros(shape_state + (HEAD_SIZE,), jnp.float32),
    )
    piece = lax.all_gather(arrived, ("role", "rep"), axis=0, tiled=True)
    count = piece.shape[0]
    visible = owner_rows[None, :] == request_ids[:, None]
    span_state = combine_states(
        initial, partial_state(query_heads, piece.reshape(count, kv_local, 2, HEAD_SIZE), visible)
    )
    row_max, totals, weighted = combine_states(cache_state, span_state)
    result = weighted / totals[..., None]
    return result.reshape(request_count, qd_width).astype(jnp.bfloat16)


def solution(mesh):
    placed = (
        P(("role", "rep"), "tp"),
        P("tp", None),
        P(("role", "rep"), "tp"),
        P(("role", "rep"), "tp"),
        P(("role", "rep"), None),
        P(("role", "rep")),
        P(),
    )
    return jax.shard_map(
        local, mesh=mesh, in_specs=placed, out_specs=P(("role", "rep"), "tp"), check_vma=False
    )
```

profile of v0, /device:TPU:0, one launch (start us, length us, event | category | flops | bytes accessed | tf_op | source)
XLA Modules:
  0.0 174.3 jit_solution(10050004590314630208)
XLA Ops:
  6.5 0.0 copy-start
  6.5 0.0 reduce-scatter.2.cloned.1.call-start
  6.5 1.6 copy-done
  8.1 9.4 %fusion.58 = f32[512,2048]{1,0:T(8,128)} fusion(bf16[512,2048]{1,0:T(8,128)(2,1)S(1)} %copy-done, bf16[2048,2048]{1,0:T(8,128)(2,1)} %param.8), kind=kOutput, calls=%fused_computation.60 | convolution fusion | flops 4294967296 | bytes 14680064 | tf_op jit(solution)/shard_map/dot_general | solution.py:61
  17.5 0.0 copy-start.5
  17.5 0.0 copy-start.3
  17.5 0.0 reduce-scatter.2.cloned.1.call-update
  17.5 0.0 all-gather.2.cloned.1.call-start
  17.6 79.6 %reduce-scatter.2.cloned.1.call-done = f32[128,2048]{1,0:T(8,128)} async-done(((f32[512,2048]{1,0:T(8,128)}), f32[128,2048]{1,0:T(8,128)}) %reduce-scatter.2.cloned.1.call-update) | async-done | bytes 1048592 | tf_op jit(solution)/shard_map/reduce_scatter | solution.py:60
  97.1 1.3 convert_element_type.16
  98.5 18.7 %all_to_all.15 = bf16[128,4,512]{2,0,1:T(8,128)(2,1)} all-to-all(bf16[128,4,512]{2,0,1:T(8,128)(2,1)S(1)} %bitcast.115), channel_id=1, replica_groups=mesh['role'=4,'rep'=2,'tp'=4] {'tp'}, dimensions={1} | all-to-all | bytes 1048576 | tf_op jit(solution)/shard_map/all_to_all | solution.py:70
  117.1 0.0 all-gather.2.cloned.1.call-update
  117.2 0.0 copy-done.5
  117.2 0.1 broadcast_bitcast_fusion
  117.2 0.0 copy-done.3
  117.3 0.0 copy-start.6
  117.3 0.0 copy-start.4
  117.3 6.8 %copy.37 = bf16[4608,512]{0,1:T(8,128)(2,1)} copy(bf16[4608,512]{1,0:T(8,128)(2,1)} %param.10) | data formatting | bytes 9437184 | tf_op args[3]
  124.1 0.1 iota_add_fusion
  124.1 0.0 copy-done.6
  124.1 0.1 broadcast_compare_fusion.1
  124.2 0.0 copy-done.4
  124.2 0.5 and_reduce_fusion
  124.8 2.6 %fusion.57 = (f32[16,2,8]{0,2,1:T(8,128)S(1)}, f32[16,2,8,4608]{3,0,2,1:T(8,128)S(1)}) fusion(bf16[16,2,8,128]{3,2,1,0:T(8,128)(2,1)S(1)} %bitcast.119, bf16[4608,2,2,128]{0,3,2,1:T(8,128)(2,1)} %bitcast.105, pred[16,4608]{1,0:T(8,128)(4,1)S(1)} %copy_bitcast_fusion.1), kind=kOutput, calls=%fused_computation.59 | convolution fusion | flops 305528576 | bytes 7218176 | tf_op jit(solution)/shard_map/rhgd,nhd->rhgn/dot_general | solution.py:26
  127.4 0.0 copy-start.1
  127.5 2.2 %copy-done.1 = f32[16,2,8,4608]{3,0,2,1:T(8,128)} copy-done((f32[16,2,8,4608]{3,0,2,1:T(8,128)}, f32[16,2,8,4608]{3,0,2,1:T(8,128)S(1)}, u32[]{:S(2)}) %copy-start.1) | copy-done | bytes 4718616
  129.6 1.1 fusion.4
  130.7 0.1 broadcast_compare_fusion
  130.8 22.2 %all-gather.2.cloned.1.call-done = bf16[4096,512]{1,0:T(8,128)(2,1)} async-done(((bf16[512,512]{1,0:T(8,128)(2,1)}), bf16[4096,512]{1,0:T(8,128)(2,1)}) %all-gather.2.cloned.1.call-update) | async-done | bytes 4194320 | tf_op jit(solution)/shard_map/all_gather | solution.py:92
  153.1 6.4 %copy.42 = bf16[4096,512]{0,1:T(8,128)(2,1)} copy(bf16[4096,512]{1,0:T(8,128)(2,1)} %all-gather.2.cloned.1.call-done) | data formatting | bytes 8388608 | tf_op jit(solution)/shard_map/all_gather | solution.py:92
  159.4 0.0 copy-start.2
  159.4 2.7 %fusion.56 = (f32[16,2,8]{0,2,1:T(8,128)S(1)}, f32[16,2,8,4096]{3,0,2,1:T(8,128)S(1)}) fusion(bf16[16,2,8,128]{3,2,1,0:T(8,128)(2,1)S(1)} %bitcast.120, bf16[4096,2,2,128]{0,3,2,1:T(8,128)(2,1)} %bitcast.111, pred[16,4096]{1,0:T(8,128)(4,1)S(1)} %broadcast_compare_fusion), kind=kOutput, calls=%fused_computation.58 | convolution fusion | flops 271580928 | bytes 6423552 | tf_op jit(solution)/shard_map/rhgd,nhd->rhgn/dot_general | solution.py:26
  162.1 0.0 slice-start
  162.1 0.0 slice-start.2
  162.1 1.0 fusion.6
  163.2 0.0 copy-done.2
  163.2 0.0 slice-start.1
  163.2 0.0 slice-start.3
  163.2 0.9 fusion.36
  164.1 0.3 slice-done
  164.4 1.2 slice-done.2
  165.5 0.2 slice-done.1
  165.8 0.1 slice-done.3
  165.9 0.9 fusion.42
  166.8 0.6 copy.76
  (11 shorter events, 0.2 us)
Async XLA Ops:
  6.5 1.6 copy-start
  6.5 90.6 %reduce-scatter.2.cloned.1.call-start = ((), (), s32[]{:S(2)}) async-start(), calls=%async_computation.2 | async-start | bytes 5242880 | tf_op jit(solution)/shard_map/reduce_scatter | solution.py:60
  17.5 99.7 %copy-start.5 = (s32[8]{0:T(128)S(1)}, s32[8]{0:T(128)}, u32[]{:S(2)}) copy-start(s32[8]{0:T(128)} %param.13) | copy-start | bytes 100
  17.5 99.8 %copy-start.3 = (bf16[16,2048]{1,0:T(8,128)(2,1)S(1)}, bf16[16,2048]{1,0:T(8,128)(2,1)}, u32[]{:S(2)}) copy-start(bf16[16,2048]{1,0:T(8,128)(2,1)} %param.9) | copy-start | bytes 196612
  17.5 135.5 %all-gather.2.cloned.1.call-start = ((), (), s32[]{:S(2)}) async-start(), calls=%async_computation.3 | async-start | bytes 4718592 | tf_op jit(solution)/shard_map/all_gather | solution.py:92
  117.3 6.9 %copy-start.6 = (s32[16]{0:T(128)S(1)}, s32[16]{0:T(128)}, u32[]{:S(2)}) copy-start(s32[16]{0:T(128)} %param.12) | copy-start | bytes 196
  117.3 6.9 %copy-start.4 = (s32[16,4]{0,1:T(4,128)S(1)}, s32[16,4]{0,1:T(4,128)}, u32[]{:S(2)}) copy-start(s32[16,4]{0,1:T(4,128)} %param.11) | copy-start | bytes 772
  127.4 2.2 %copy-start.1 = (f32[16,2,8,4608]{3,0,2,1:T(8,128)}, f32[16,2,8,4608]{3,0,2,1:T(8,128)S(1)}, u32[]{:S(2)}) copy-start(f32[16,2,8,4608]{3,0,2,1:T(8,128)S(1)} %get-tuple-element.16) | copy-start | bytes 14155780
  159.4 3.7 %copy-start.2 = (bf16[4096,512]{0,1:T(8,128)(2,1)S(1)}, bf16[4096,512]{0,1:T(8,128)(2,1)}, u32[]{:S(2)}) copy-start(bf16[4096,512]{0,1:T(8,128)(2,1)} %copy.42) | copy-start | bytes 12582916
  162.1 2.2 %slice-start = ((s8[4718592]{0:T(1024)(128)(4,1)}), s8[4194304]{0:T(1024)(128)(4,1)S(1)}, s32[]{:S(2)}) async-start(s8[4718592]{0:T(1024)(128)(4,1)} %bitcast.106), calls=%async_computation.4 | async-start | bytes 8388608
  162.1 3.4 %slice-start.2 = ((s8[4718592]{0:T(1024)(128)(4,1)}), s8[4194304]{0:T(1024)(128)(4,1)S(1)}, s32[]{:S(2)}) async-start(s8[4718592]{0:T(1024)(128)(4,1)} %bitcast.109), calls=%async_computation.6 | async-start | bytes 8388608
  163.2 2.6 %slice-start.1 = ((s8[4718592]{0:T(1024)(128)(4,1)}), s8[524288]{0:T(1024)(128)(4,1)S(1)}, s32[]{:S(2)}) async-start(s8[4718592]{0:T(1024)(128)(4,1)} %bitcast.106), calls=%async_computation.5 | async-start | bytes 1048576
  163.2 2.8 %slice-start.3 = ((s8[4718592]{0:T(1024)(128)(4,1)}), s8[524288]{0:T(1024)(128)(4,1)S(1)}, s32[]{:S(2)}) async-start(s8[4718592]{0:T(1024)(128)(4,1)} %bitcast.109), calls=%async_computation.7 | async-start | bytes 1048576
Sparse Core Ops, SparseCore 0:
  17.6 79.4 reduce-scatter.1
  117.3 35.7 all-gather.1
where the time goes:
time: 175 us; the launch traced here: 174 us
  waiting for transfers between devices  102 us (58%)
  local copies, waits for them, and re-layouts  19.6 us (11%)
  blocking collectives  18.7 us (11%)
  matrix products  16.4 us (9%)
  between operations  13.6 us (8%)
  other arithmetic  4.16 us (2%)
    reduce_scatter x1, waiting for transfers between devices, local(): lax.psum_scatter(jnp.dot(span_hidden, key_value_weight, preferred_element...  79.6 us
    all_gather x1, waiting for transfers between devices, local(): piece = lax.all_gather(arrived, ('role', 'rep'), axis=0, tiled=True)  22.2 us
    all_to_all x1, blocking collectives, local(): lax.all_to_all(outgoing, 'tp', split_axis=1, concat_axis=0, tiled=True)  18.7 us
    unnamed x27, local copies, waits for them, and re-layouts  13.1 us
    dot_general x1, matrix products, local(): jnp.dot(span_hidden, key_value_weight, preferred_element_type=jnp.float32)  9.36 us
    all_gather x1, local copies, waits for them, and re-layouts, local(): piece = lax.all_gather(arrived, ('role', 'rep'), axis=0, tiled=True)  6.39 us
    dot_general x2, matrix products, partial_state(): jnp.einsum('rhgd,nhd->rhgn', query_heads, kv_rows[:, :, 0], preferred_ele...  5.33 us
  transfers between devices with their start and end apart: 2, of which 2 were waited for; matrix products, arithmetic and copies ran while one was open for 7% of the time, Pallas kernels for 0%

commit v1 on v0

v1 whole, which is shorter than its diff:
```python
import functools

import jax
import jax.numpy as jnp
from jax import lax
from jax.experimental import pallas as pl
from jax.experimental.pallas import tpu as pltpu
from jax.sharding import PartitionSpec as P

HEAD_SIZE = 128
PAGE_TOKENS = 128
MESH = pl.DeviceIdType.MESH
HIDDEN = -1e30
CHUNKS = 4
NT = (((1,), (1,)), ((), ()))
NN = (((1,), (0,)), ((), ()))


def dot(a, b, dims):
    return lax.dot_general(a, b, dims, preferred_element_type=jnp.float32)


def split(value):
    high = value.astype(jnp.bfloat16)
    return high, (value - high.astype(jnp.float32)).astype(jnp.bfloat16)


def spread(rows, heads):
    if heads == 1:
        return rows
    each = rows.shape[0] // heads
    owner = lax.broadcasted_iota(jnp.int32, rows.shape, 0) // each
    wide = rows.astype(jnp.float32)
    parts = [jnp.where(owner == h, wide, 0.0) for h in range(heads)]
    return jnp.concatenate(parts, axis=1).astype(jnp.bfloat16)


def gather_blocks(rows, heads):
    if heads == 1:
        return rows
    each = rows.shape[0] // heads
    shape = (rows.shape[0], HEAD_SIZE)
    owner = lax.broadcasted_iota(jnp.int32, shape, 0) // each
    result = rows[:, :HEAD_SIZE]
    for h in range(1, heads):
        result = jnp.where(owner == h, rows[:, h * HEAD_SIZE:(h + 1) * HEAD_SIZE], result)
    return result


def kernel(
    sizes,
    placement, table, lengths, q_ref, x_hbm, w_hbm, cache_hbm,
    out_ref,
    x_v, w_v, cache_v, chosen, q_land, q_all, qt, s_part, s_land, p_all, ub, o_part, o_land,
    state, c_out, c_max, c_sum,
    local_sem, a_send, a_recv, t_send, t_recv, e_send, e_recv,
):
    n_role, n_rep, n_tp = sizes
    n_replica = n_role * n_rep
    scale = HEAD_SIZE ** -0.5
    requests, rows = q_ref.shape[0], q_ref.shape[1]
    features = x_v.shape[1]
    local_heads = cache_v.shape[2] // (2 * HEAD_SIZE)
    pairs = w_v.shape[1] // (4 * HEAD_SIZE)
    pair_rows = n_tp * rows // pairs
    pair_slots = pair_rows // rows
    piece = features // CHUNKS
    slots = table.shape[1]

    replica = lax.axis_index("role") * n_rep + lax.axis_index("rep")
    t = lax.axis_index("tp")

    def on_replica(i):
        return (i // n_rep, lax.rem(i, n_rep), t)

    def on_tp(i):
        return (lax.axis_index("role"), lax.axis_index("rep"), i)

    def others(me, count):
        return [(d, lax.rem(me + d, count)) for d in range(1, count)]

    replicas = others(replica, n_replica)
    columns = others(t, n_tp)

    half = cache_v.shape[0] // 2
    cache_copies = [
        pltpu.make_async_copy(
            cache_hbm.at[pl.ds(h * half, half)], cache_v.at[pl.ds(h * half, half)], local_sem.at[h]
        )
        for h in range(2)
    ]
    w_copies = [
        pltpu.make_async_copy(
            w_hbm.at[pl.ds(c * piece, piece)], w_v.at[pl.ds(c * piece, piece)], local_sem.at[2 + c]
        )
        for c in range(CHUNKS)
    ]
    x_copy = pltpu.make_async_copy(x_hbm, x_v, local_sem.at[2 + CHUNKS])
    for copy in cache_copies + w_copies + [x_copy]:
        copy.start()

    barrier = pltpu.get_barrier_semaphore()
    for _, i in replicas:
        pl.semaphore_signal(barrier, inc=1, device_id=on_replica(i), device_id_type=MESH)
    for _, i in columns:
        pl.semaphore_signal(barrier, inc=1, device_id=on_tp(i), device_id_type=MESH)
    for i in range(n_replica):
        chosen[i] = q_ref[lax.rem(placement[i], requests)]
    pl.semaphore_wait(barrier, n_replica + n_tp - 2)

    pending = []

    def send(source, land, slot, peers, device, send_sem, recv_sem):
        for d, i in peers:
            copy = pltpu.make_async_remote_copy(
                src_ref=source(i), dst_ref=land.at[slot],
                send_sem=send_sem.at[d], recv_sem=recv_sem.at[slot],
                device_id=device(i), device_id_type=MESH,
            )
            copy.start()
            pending.append(copy)

    def receive(land, peers, device, send_sem, recv_sem):
        for d, i in peers:
            pltpu.make_async_remote_copy(
                src_ref=land.at[i], dst_ref=land.at[i],
                send_sem=send_sem.at[d], recv_sem=recv_sem.at[i],
                device_id=device(i), device_id_type=MESH,
            ).wait_recv()

    send(lambda i: chosen.at[i], q_land, replica, replicas, on_replica, a_send, a_recv)
    q_land[replica] = chosen[replica]

    def cache_request(k):
        blocks = [
            cache_v[table[k, j]]
            for j in range(slots)
        ]
        block = jnp.concatenate(blocks, axis=0)

        def take(which):
            return jnp.concatenate(
                [
                    block[:, (2 * h + which) * HEAD_SIZE:(2 * h + which + 1) * HEAD_SIZE]
                    for h in range(local_heads)
                ],
                axis=1,
            )

        scores = dot(spread(q_ref[k], local_heads), take(0), NT) * scale
        seen = lax.broadcasted_iota(jnp.int32, scores.shape, 1) < lengths[k]
        scores = jnp.where(seen, scores, HIDDEN)
        top = jnp.max(scores, axis=1, keepdims=True)
        probs = jnp.where(seen, jnp.exp(scores - top), 0.0)
        total = jnp.sum(probs, axis=1, keepdims=True)
        summed = dot(probs.astype(jnp.bfloat16), take(1), NN)
        c_out[k] = gather_blocks(summed, local_heads)
        c_max[k] = jnp.broadcast_to(top, (rows, HEAD_SIZE))
        c_sum[k] = jnp.broadcast_to(total, (rows, HEAD_SIZE))

    def cache_part(first, last):
        def body(step, carry):
            for u in range(2):
                cache_request(first + 2 * step + u)
            return carry

        lax.fori_loop(0, (last - first) // 2, body, 0)

    for copy in cache_copies:
        copy.wait()
    cache_part(0, requests // 2)

    receive(q_land, replicas, on_replica, a_send, a_recv)
    q_all[t] = q_land[lax.div(placement[replica], requests)]
    send(lambda i: q_all.at[t], q_all, t, columns, on_tp, t_send.at[0], t_recv.at[0])
    cache_part(requests // 2, 3 * requests // 4)
    receive(q_all, columns, on_tp, t_send.at[0], t_recv.at[0])

    pair_q = q_all[...].reshape(pairs, pair_rows, HEAD_SIZE)
    wide_q = [spread(pair_q[g], 2) for g in range(pairs)]

    def weight(rows_at, g, which):
        left = (4 * g + which) * HEAD_SIZE
        right = (4 * g + 2 + which) * HEAD_SIZE
        return jnp.concatenate(
            [w_v[rows_at, left:left + HEAD_SIZE], w_v[rows_at, right:right + HEAD_SIZE]], axis=1
        )

    for c in range(CHUNKS):
        w_copies[c].wait()
        at = pl.ds(c * piece, piece)
        for g in range(pairs):
            high, low = split(dot(wide_q[g], weight(at, g, 0), NT))
            qt[g, 0, :, at] = high
            qt[g, 1, :, at] = low
    x_copy.wait()
    both = dot(qt[...].reshape(pairs * 2 * pair_rows, features), x_v[...], NT)
    tokens = both.shape[1]
    both = both.reshape(pairs, 2, pair_rows, tokens)
    s_part[...] = (both[:, 0] + both[:, 1]).reshape(n_tp, rows, tokens)
    send(lambda i: s_part.at[i], s_land, t, columns, on_tp, t_send.at[1], t_recv.at[1])
    cache_part(3 * requests // 4, requests)
    receive(s_land, columns, on_tp, t_send.at[1], t_recv.at[1])

    scores = s_part[t]
    for _, i in columns:
        scores = scores + s_land[i]
    scores = scores * scale
    top = jnp.max(scores, axis=1, keepdims=True)
    probs = jnp.exp(scores - top)
    p_all[t] = probs.astype(jnp.bfloat16)
    send(lambda i: p_all.at[t], p_all, t, columns, on_tp, t_send.at[2], t_recv.at[2])
    state[replica, 1] = jnp.broadcast_to(top, (rows, HEAD_SIZE))
    state[replica, 2] = jnp.broadcast_to(jnp.sum(probs, axis=1, keepdims=True), (rows, HEAD_SIZE))
    receive(p_all, columns, on_tp, t_send.at[2], t_recv.at[2])

    weights = p_all[...].reshape(n_tp * rows, tokens)
    for c in range(CHUNKS):
        at = pl.ds(c * piece, piece)
        high, low = split(dot(weights, x_v[:, at], NN))
        ub[:, 0, :, at] = high.reshape(pairs, pair_rows, piece)
        ub[:, 1, :, at] = low.reshape(pairs, pair_rows, piece)
    for g in range(pairs):
        both = dot(ub[g].reshape(2 * pair_rows, features), weight(slice(None), g, 1), NN)
        both = gather_blocks(both[:pair_rows] + both[pair_rows:], 2)
        o_part[g * pair_slots:(g + 1) * pair_slots] = both.reshape(pair_slots, rows, HEAD_SIZE)
    send(lambda i: o_part.at[i], o_land, t, columns, on_tp, t_send.at[3], t_recv.at[3])
    receive(o_land, columns, on_tp, t_send.at[3], t_recv.at[3])
    summed = o_part[t]
    for _, i in columns:
        summed = summed + o_land[i]
    state[replica, 0] = summed

    send(lambda i: state.at[replica], state, replica, replicas, on_replica, e_send, e_recv)
    receive(state, replicas, on_replica, e_send, e_recv)

    def combine(k, carry):
        request = jnp.full((rows, HEAD_SIZE), replica * requests + k, jnp.int32)
        hits = [request == placement[i] for i in range(n_replica)]
        top = c_max[k]
        for i in range(n_replica):
            top = jnp.maximum(top, jnp.where(hits[i], state[i, 1], HIDDEN))
        factor = jnp.exp(c_max[k] - top)
        summed = c_out[k] * factor
        total = c_sum[k] * factor
        for i in range(n_replica):
            factor = jnp.where(hits[i], jnp.exp(state[i, 1] - top), 0.0)
            summed = summed + state[i, 0] * factor
            total = total + state[i, 2] * factor
        out_ref[k] = (summed / total).astype(out_ref.dtype)
        return carry

    lax.fori_loop(0, requests, combine, 0)
    for copy in pending:
        copy.wait_send()


def local(sizes, span_hidden, key_value_weight, queries, kv_cache, block_table, lengths, placement):
    n_role, n_rep, n_tp = sizes
    n_replica = n_role * n_rep
    requests = queries.shape[0]
    heads = queries.shape[1] // HEAD_SIZE
    rows = max(heads, 16)
    tokens, features = span_hidden.shape
    pairs = key_value_weight.shape[1] // (4 * HEAD_SIZE)
    pair_rows = n_tp * rows // pairs
    pool = kv_cache.reshape(-1, PAGE_TOKENS, kv_cache.shape[1])
    q = queries.reshape(requests, heads, HEAD_SIZE)
    if rows > heads:
        q = jnp.pad(q, ((0, 0), (0, rows - heads), (0, 0)))
    bf16, f32 = jnp.bfloat16, jnp.float32
    smem = pl.BlockSpec(memory_space=pltpu.SMEM)
    vmem = pl.BlockSpec(memory_space=pltpu.VMEM)
    hbm = pl.BlockSpec(memory_space=pl.ANY)
    dma = pltpu.SemaphoreType.DMA
    out = pl.pallas_call(
        functools.partial(kernel, sizes),
        out_shape=jax.ShapeDtypeStruct((requests, rows, HEAD_SIZE), bf16),
        in_specs=[smem, smem, smem, vmem, hbm, hbm, hbm],
        out_specs=vmem,
        scratch_shapes=[
            pltpu.VMEM(span_hidden.shape, bf16),
            pltpu.VMEM(key_value_weight.shape, bf16),
            pltpu.VMEM(pool.shape, bf16),
            pltpu.VMEM((n_replica, rows, HEAD_SIZE), bf16),
            pltpu.VMEM((n_replica, rows, HEAD_SIZE), bf16),
            pltpu.VMEM((n_tp, rows, HEAD_SIZE), bf16),
            pltpu.VMEM((pairs, 2, pair_rows, features), bf16),
            pltpu.VMEM((n_tp, rows, tokens), f32),
            pltpu.VMEM((n_tp, rows, tokens), f32),
            pltpu.VMEM((n_tp, rows, tokens), bf16),
            pltpu.VMEM((pairs, 2, pair_rows, features), bf16),
            pltpu.VMEM((n_tp, rows, HEAD_SIZE), f32),
            pltpu.VMEM((n_tp, rows, HEAD_SIZE), f32),
            pltpu.VMEM((n_replica, 3, rows, HEAD_SIZE), f32),
            pltpu.VMEM((requests, rows, HEAD_SIZE), f32),
            pltpu.VMEM((requests, rows, HEAD_SIZE), f32),
            pltpu.VMEM((requests, rows, HEAD_SIZE), f32),
            dma((3 + CHUNKS,)),
            dma((n_replica,)),
            dma((n_replica,)),
            dma((4, n_tp)),
            dma((4, n_tp)),
            dma((n_replica,)),
            dma((n_replica,)),
        ],
        compiler_params=pltpu.CompilerParams(
            collective_id=0, has_side_effects=True, vmem_limit_bytes=60 * 1024 * 1024
        ),
    )(placement, block_table, lengths, q, span_hidden, key_value_weight, pool)
    return out[:, :heads].reshape(requests, heads * HEAD_SIZE)


def solution(mesh):
    placed = (
        P(("role", "rep"), "tp"),
        P("tp", None),
        P(("role", "rep"), "tp"),
        P(("role", "rep"), "tp"),
        P(("role", "rep"), None),
        P(("role", "rep")),
        P(),
    )
    sizes = (mesh.shape["role"], mesh.shape["rep"], mesh.shape["tp"])
    return jax.shard_map(
        functools.partial(local, sizes),
        mesh=mesh, in_specs=placed, out_specs=P(("role", "rep"), "tp"), check_vma=False,
    )
```

time: 175 us -> 38.7 us (0.22)
  waiting for transfers between devices: 102 us -> 0 us
  Pallas kernels: 0 us -> 34.1 us
  blocking collectives: 18.7 us -> 0 us
  matrix products: 16.4 us -> 0 us
  local copies, waits for them, and re-layouts: 19.6 us -> 4.31 us
  between operations: 13.6 us -> 0.01 us
  other arithmetic: 4.16 us -> 0 us
    reduce_scatter x1 -> x0, waiting for transfers between devices: 79.6 us -> none  [local(): lax.psum_scatter(jnp.dot(span_hidden, key_value_weight, preferred_element...]
    pallas_call x0 -> x1, Pallas kernels: none -> 34.1 us  [local(): pl.pallas_call(functools.partial(kernel, sizes), out_shape=jax.ShapeDtype...]
    all_gather x1 -> x0, waiting for transfers between devices: 22.2 us -> none  [local(): piece = lax.all_gather(arrived, ('role', 'rep'), axis=0, tiled=True)]
    all_to_all x1 -> x0, blocking collectives: 18.7 us -> none  [local(): lax.all_to_all(outgoing, 'tp', split_axis=1, concat_axis=0, tiled=True)]
    dot_general x5 -> x0, matrix products: 16.4 us -> none  [the longest x1 9.36 us: local(): jnp.dot(span_hidden, key_value_weight, preferred_element_type=jnp.float32)]
    unnamed x27 -> x3, local copies, waits for them, and re-layouts: 13.1 us -> 4.31 us
    all_gather x1 -> x0, local copies, waits for them, and re-layouts: 6.39 us -> none  [local(): piece = lax.all_gather(arrived, ('role', 'rep'), axis=0, tiled=True)]
    reduce_sum x2 -> x0, other arithmetic: 2.06 us -> none  [partial_state(): totals = jnp.sum(probs, axis=-1)]
  transfers between devices with their start and end apart: 2 -> 0, of which waited for: 2 -> 0; matrix products, arithmetic and copies ran while one was open for 7% -> 0% of each run, Pallas kernels for 0% -> 0%
where the time goes in v1:
time: 38.7 us; the launch traced here: 38.4 us
  Pallas kernels  34.1 us (88%)
  local copies, waits for them, and re-layouts  4.31 us (11%)
    pallas_call x1, Pallas kernels, local(): pl.pallas_call(functools.partial(kernel, sizes), out_shape=jax.ShapeDtype...  34.1 us
    unnamed x3, local copies, waits for them, and re-layouts  4.31 us

profile of v1, /device:TPU:0, one launch (start us, length us, event | category | flops | bytes accessed | tf_op | source)
XLA Modules:
  0.0 38.4 jit_solution(685377599386906091)
XLA Ops:
  0.0 1.3 %copy.8.table = s32[16,4]{1,0:T(8,128)} copy(s32[16,4]{0,1:T(4,128)} %param.11) | data formatting | bytes 512 | tf_op args[4]
  1.4 1.5 %copy.9 = bf16[2,8,16,128]{3,2,1,0:T(8,128)(2,1)} copy(bf16[2,8,16,128]{3,1,2,0:T(8,128)(2,1)} %bitcast.10) | data formatting | bytes 131072
  2.8 34.1 %shard_map.73 = bf16[16,16,128]{2,1,0:T(8,128)(2,1)} custom-call(s32[8]{0:T(128)} %placement.1, s32[16,4]{1,0:T(8,128)} %copy.8.table, s32[16]{0:T(128)} %lengths.1, bf16[16,16,128]{2,1,0:T(8,128)(2,1)} %bitcast.9, bf16[512,2048]{1,0:T(8,128)(2,1)} %x_hbm.1, bf16[2048,2048]{1,0:T(8,128)(2,1)} %w_hbm.1, bf16[36,128,512]{2,1,0:T(8,128)(2,1)} %bitcast.7), custom_call_target="tpu_custom_call" | custom-call | tf_op jit(solution)/shard_map/pallas_call | solution.py:276
  36.9 1.5 %copy.12 = bf16[2,8,16,128]{3,1,2,0:T(8,128)(2,1)} copy(bf16[2,8,16,128]{3,2,1,0:T(8,128)(2,1)} %bitcast.8) | data formatting | bytes 131072

commit v2 on v1

--- a/solution.py
+++ b/solution.py
@@ -51,21 +51,22 @@
     sizes,
     placement, table, lengths, q_ref, x_hbm, w_hbm, cache_hbm,
     out_ref,
-    x_v, w_v, cache_v, chosen, q_land, q_all, qt, s_part, s_land, p_all, ub, o_part, o_land,
-    state, c_out, c_max, c_sum,
-    local_sem, a_send, a_recv, t_send, t_recv, e_send, e_recv,
+    x_v, w_v, cache_v, q_rows, chosen, q_land, q_all, qt, s_part, s_land, p_all, ub, o_part, o_land,
+    state, marks, c_out, c_max, c_sum,
+    local_sem, a_send, a_recv, t_send, t_recv, m_send, m_recv, e_send, e_recv,
 ):
     n_role, n_rep, n_tp = sizes
     n_replica = n_role * n_rep
     scale = HEAD_SIZE ** -0.5
-    requests, rows = q_ref.shape[0], q_ref.shape[1]
+    requests, rows = q_rows.shape[0], q_rows.shape[1]
+    heads = q_ref.shape[1] // HEAD_SIZE
     features = x_v.shape[1]
     local_heads = cache_v.shape[2] // (2 * HEAD_SIZE)
     pairs = w_v.shape[1] // (4 * HEAD_SIZE)
     pair_rows = n_tp * rows // pairs
     pair_slots = pair_rows // rows
     piece = features // CHUNKS
-    slots = table.shape[1]
+    slots = table.shape[0]
 
     replica = lax.axis_index("role") * n_rep + lax.axis_index("rep")
     t = lax.axis_index("tp")
@@ -82,6 +83,11 @@
     replicas = others(replica, n_replica)
     columns = others(t, n_tp)
 
+    barrier = pltpu.get_barrier_semaphore()
+    for _, i in replicas:
+        pl.semaphore_signal(barrier, inc=1, device_id=on_replica(i), device_id_type=MESH)
+    for _, i in columns:
+        pl.semaphore_signal(barrier, inc=1, device_id=on_tp(i), device_id_type=MESH)
     half = cache_v.shape[0] // 2
     cache_copies = [
         pltpu.make_async_copy(
@@ -99,13 +105,12 @@
     for copy in cache_copies + w_copies + [x_copy]:
         copy.start()
 
-    barrier = pltpu.get_barrier_semaphore()
-    for _, i in replicas:
-        pl.semaphore_signal(barrier, inc=1, device_id=on_replica(i), device_id_type=MESH)
-    for _, i in columns:
-        pl.semaphore_signal(barrier, inc=1, device_id=on_tp(i), device_id_type=MESH)
+    if rows > heads:
+        q_rows[...] = jnp.zeros_like(q_rows)
+    for h in range(heads):
+        q_rows[:, h, :] = q_ref[:, h * HEAD_SIZE:(h + 1) * HEAD_SIZE].astype(jnp.float32)
     for i in range(n_replica):
-        chosen[i] = q_ref[lax.rem(placement[i], requests)]
+        chosen[i] = q_rows[lax.rem(placement[i], requests)].astype(jnp.bfloat16)
     pl.semaphore_wait(barrier, n_replica + n_tp - 2)
 
     pending = []
@@ -133,7 +138,7 @@
 
     def cache_request(k):
         blocks = [
-            cache_v[table[k, j]]
+            cache_v[table[j, k]]
             for j in range(slots)
         ]
         block = jnp.concatenate(blocks, axis=0)
@@ -147,7 +152,7 @@
                 axis=1,
             )
 
-        scores = dot(spread(q_ref[k], local_heads), take(0), NT) * scale
+        scores = dot(spread(q_rows[k].astype(jnp.bfloat16), local_heads), take(0), NT) * scale
         seen = lax.broadcasted_iota(jnp.int32, scores.shape, 1) < lengths[k]
         scores = jnp.where(seen, scores, HIDDEN)
         top = jnp.max(scores, axis=1, keepdims=True)
@@ -210,8 +215,9 @@
     probs = jnp.exp(scores - top)
     p_all[t] = probs.astype(jnp.bfloat16)
     send(lambda i: p_all.at[t], p_all, t, columns, on_tp, t_send.at[2], t_recv.at[2])
-    state[replica, 1] = jnp.broadcast_to(top, (rows, HEAD_SIZE))
-    state[replica, 2] = jnp.broadcast_to(jnp.sum(probs, axis=1, keepdims=True), (rows, HEAD_SIZE))
+    marks[replica, 0] = jnp.broadcast_to(top, (rows, HEAD_SIZE))
+    marks[replica, 1] = jnp.broadcast_to(jnp.sum(probs, axis=1, keepdims=True), (rows, HEAD_SIZE))
+    send(lambda i: marks.at[replica], marks, replica, replicas, on_replica, m_send, m_recv)
     receive(p_all, columns, on_tp, t_send.at[2], t_recv.at[2])
 
     weights = p_all[...].reshape(n_tp * rows, tokens)
@@ -229,9 +235,10 @@
     summed = o_part[t]
     for _, i in columns:
         summed = summed + o_land[i]
-    state[replica, 0] = summed
+    state[replica] = summed
 
     send(lambda i: state.at[replica], state, replica, replicas, on_replica, e_send, e_recv)
+    receive(marks, replicas, on_replica, m_send, m_recv)
     receive(state, replicas, on_replica, e_send, e_recv)
 
     def combine(k, carry):
@@ -239,18 +246,20 @@
         hits = [request == placement[i] for i in range(n_replica)]
         top = c_max[k]
         for i in range(n_replica):
-            top = jnp.maximum(top, jnp.where(hits[i], state[i, 1], HIDDEN))
+            top = jnp.maximum(top, jnp.where(hits[i], marks[i, 0], HIDDEN))
         factor = jnp.exp(c_max[k] - top)
         summed = c_out[k] * factor
         total = c_sum[k] * factor
         for i in range(n_replica):
-            factor = jnp.where(hits[i], jnp.exp(state[i, 1] - top), 0.0)
-            summed = summed + state[i, 0] * factor
-            total = total + state[i, 2] * factor
-        out_ref[k] = (summed / total).astype(out_ref.dtype)
+            factor = jnp.where(hits[i], jnp.exp(marks[i, 0] - top), 0.0)
+            summed = summed + state[i] * factor
+            total = total + marks[i, 1] * factor
+        c_out[k] = summed / total
         return carry
 
     lax.fori_loop(0, requests, combine, 0)
+    for h in range(heads):
+        out_ref[:, h * HEAD_SIZE:(h + 1) * HEAD_SIZE] = c_out[:, h, :].astype(out_ref.dtype)
     for copy in pending:
         copy.wait_send()
 
@@ -265,23 +274,21 @@
     pairs = key_value_weight.shape[1] // (4 * HEAD_SIZE)
     pair_rows = n_tp * rows // pairs
     pool = kv_cache.reshape(-1, PAGE_TOKENS, kv_cache.shape[1])
-    q = queries.reshape(requests, heads, HEAD_SIZE)
-    if rows > heads:
-        q = jnp.pad(q, ((0, 0), (0, rows - heads), (0, 0)))
     bf16, f32 = jnp.bfloat16, jnp.float32
     smem = pl.BlockSpec(memory_space=pltpu.SMEM)
     vmem = pl.BlockSpec(memory_space=pltpu.VMEM)
     hbm = pl.BlockSpec(memory_space=pl.ANY)
     dma = pltpu.SemaphoreType.DMA
-    out = pl.pallas_call(
+    return pl.pallas_call(
         functools.partial(kernel, sizes),
-        out_shape=jax.ShapeDtypeStruct((requests, rows, HEAD_SIZE), bf16),
+        out_shape=jax.ShapeDtypeStruct(queries.shape, bf16),
         in_specs=[smem, smem, smem, vmem, hbm, hbm, hbm],
         out_specs=vmem,
         scratch_shapes=[
             pltpu.VMEM(span_hidden.shape, bf16),
             pltpu.VMEM(key_value_weight.shape, bf16),
             pltpu.VMEM(pool.shape, bf16),
+            pltpu.VMEM((requests, rows, HEAD_SIZE), f32),
             pltpu.VMEM((n_replica, rows, HEAD_SIZE), bf16),
             pltpu.VMEM((n_replica, rows, HEAD_SIZE), bf16),
             pltpu.VMEM((n_tp, rows, HEAD_SIZE), bf16),
@@ -292,7 +299,8 @@
             pltpu.VMEM((pairs, 2, pair_rows, features), bf16),
             pltpu.VMEM((n_tp, rows, HEAD_SIZE), f32),
             pltpu.VMEM((n_tp, rows, HEAD_SIZE), f32),
-            pltpu.VMEM((n_replica, 3, rows, HEAD_SIZE), f32),
+            pltpu.VMEM((n_replica, rows, HEAD_SIZE), f32),
+            pltpu.VMEM((n_replica, 2, rows, HEAD_SIZE), f32),
             pltpu.VMEM((requests, rows, HEAD_SIZE), f32),
             pltpu.VMEM((requests, rows, HEAD_SIZE), f32),
             pltpu.VMEM((requests, rows, HEAD_SIZE), f32),
@@ -303,12 +311,13 @@
             dma((4, n_tp)),
             dma((n_replica,)),
             dma((n_replica,)),
+            dma((n_replica,)),
+            dma((n_replica,)),
         ],
         compiler_params=pltpu.CompilerParams(
             collective_id=0, has_side_effects=True, vmem_limit_bytes=60 * 1024 * 1024
         ),
-    )(placement, block_table, lengths, q, span_hidden, key_value_weight, pool)
-    return out[:, :heads].reshape(requests, heads * HEAD_SIZE)
+    )(placement, block_table.T, lengths, queries, span_hidden, key_value_weight, pool)
 
 
 def solution(mesh):

time: 38.7 us -> 35.9 us (0.928)
  local copies, waits for them, and re-layouts: 4.31 us -> 1.47 us
    unnamed x3 -> x1, local copies, waits for them, and re-layouts: 4.31 us -> 1.47 us
where the time goes in v2:
time: 35.9 us; the launch traced here: 35.7 us
  Pallas kernels  34.2 us (95%)
  local copies, waits for them, and re-layouts  1.47 us (4%)
    pallas_call x1, Pallas kernels, local(): pl.pallas_call(functools.partial(kernel, sizes), out_shape=jax.ShapeDtype...  34.2 us
    unnamed x1, local copies, waits for them, and re-layouts  1.47 us

profile of v2, /device:TPU:0, one launch (start us, length us, event | category | flops | bytes accessed | tf_op | source)
XLA Modules:
  0.0 35.7 jit_solution(16725027563444431490)
XLA Ops:
  0.0 34.2 %shard_map.73 = bf16[16,2048]{1,0:T(8,128)(2,1)} custom-call(s32[8]{0:T(128)} %placement.1, s32[4,16]{1,0:T(4,128)} %bitcast.3, s32[16]{0:T(128)} %lengths.1, bf16[16,2048]{1,0:T(8,128)(2,1)} %q_ref.1, bf16[512,2048]{1,0:T(8,128)(2,1)} %x_hbm.1, bf16[2048,2048]{1,0:T(8,128)(2,1)} %w_hbm.1, bf16[36,128,512]{2,1,0:T(8,128)(2,1)} %bitcast.2), custom_call_target="tpu_custom_call" | custom-call | tf_op jit(solution)/shard_map/pallas_call | solution.py:282
  34.2 1.5 %copy.9 = bf16[16,2048]{1,0:T(8,128)(2,1)} copy(bf16[16,2048]{1,0:T(8,128)(2,1)} %shard_map.73) | data formatting | bytes 131072

commit v3 on v2

v3 whole, which is shorter than its diff:
```python
import functools

import jax
import jax.numpy as jnp
from jax import lax
from jax.experimental import pallas as pl
from jax.experimental.pallas import tpu as pltpu
from jax.sharding import PartitionSpec as P

HEAD_SIZE = 128
PAGE_TOKENS = 128
MESH = pl.DeviceIdType.MESH
HIDDEN = -1e30
CHUNKS = 4
NT = (((1,), (1,)), ((), ()))
NN = (((1,), (0,)), ((), ()))


def dot(a, b, dims):
    return lax.dot_general(a, b, dims, preferred_element_type=jnp.float32)


def split(value):
    high = value.astype(jnp.bfloat16)
    return high, (value - high.astype(jnp.float32)).astype(jnp.bfloat16)


def spread(rows, heads, each, first=0):
    if heads == 1:
        return rows
    owner = (lax.broadcasted_iota(jnp.int32, rows.shape, 0) + first) // each
    wide = rows.astype(jnp.float32)
    parts = [jnp.where(owner == h, wide, 0.0) for h in range(heads)]
    return jnp.concatenate(parts, axis=1).astype(jnp.bfloat16)


def gather_blocks(rows, heads, each, first=0):
    if heads == 1:
        return rows
    shape = (rows.shape[0], HEAD_SIZE)
    owner = (lax.broadcasted_iota(jnp.int32, shape, 0) + first) // each
    result = rows[:, :HEAD_SIZE]
    for h in range(1, heads):
        result = jnp.where(owner == h, rows[:, h * HEAD_SIZE:(h + 1) * HEAD_SIZE], result)
    return result


def kernel(
    sizes,
    placement, table, lengths, q_ref, x_hbm, w_hbm, cache_hbm,
    out_ref,
    x_v, w_v, cache_v, q_rows, chosen, q_land, q_all, s_part, s_land, p_all, o_part, o_land,
    state, marks, factors, c_out, c_max, c_sum,
    local_sem, a_send, a_recv, t_send, t_recv, m_send, m_recv, e_send, e_recv,
):
    n_role, n_rep, n_tp = sizes
    n_replica = n_role * n_rep
    scale = HEAD_SIZE ** -0.5
    requests, rows = q_rows.shape[0], q_rows.shape[1]
    heads = q_ref.shape[1] // HEAD_SIZE
    features = x_v.shape[1]
    local_heads = cache_v.shape[2] // (2 * HEAD_SIZE)
    pairs = w_v.shape[1] // (4 * HEAD_SIZE)
    pair_rows = n_tp * rows // pairs
    pair_slots = pair_rows // rows
    piece = features // CHUNKS
    slots = table.shape[0]

    replica = lax.axis_index("role") * n_rep + lax.axis_index("rep")
    t = lax.axis_index("tp")

    role, rep = lax.axis_index("role"), lax.axis_index("rep")

    def wrap(value, count):
        return jnp.where(value >= count, value - count, value)

    replicas = []
    for step in range(1, n_replica):
        to_role, to_rep = wrap(role + step // n_rep, n_role), wrap(rep + step % n_rep, n_rep)
        replicas.append((step, to_role * n_rep + to_rep, (to_role, to_rep, t)))
    columns = []
    for step in range(1, n_tp):
        down, up = n_tp - step, step - 1
        down = jnp.where(down <= t, down - 1, down)
        up = jnp.where(up >= t, up + 1, up)
        to_tp = jnp.where(2 * t < n_tp, down, up)
        columns.append((step, to_tp, (role, rep, to_tp)))

    barrier = pltpu.get_barrier_semaphore()
    for _, _, device in columns + replicas:
        pl.semaphore_signal(barrier, inc=1, device_id=device, device_id_type=MESH)
    half = cache_v.shape[0] // 2
    cache_copies = [
        pltpu.make_async_copy(
            cache_hbm.at[pl.ds(h * half, half)], cache_v.at[pl.ds(h * half, half)], local_sem.at[h]
        )
        for h in range(2)
    ]
    w_copies = [
        pltpu.make_async_copy(
            w_hbm.at[pl.ds(c * piece, piece)], w_v.at[pl.ds(c * piece, piece)], local_sem.at[2 + c]
        )
        for c in range(CHUNKS)
    ]
    x_copy = pltpu.make_async_copy(x_hbm, x_v, local_sem.at[2 + CHUNKS])
    for copy in cache_copies + w_copies + [x_copy]:
        copy.start()

    if rows > heads:
        q_rows[...] = jnp.zeros_like(q_rows)
    for h in range(heads):
        q_rows[:, h, :] = q_ref[:, h * HEAD_SIZE:(h + 1) * HEAD_SIZE].astype(jnp.float32)
    for i in range(n_replica):
        chosen[i] = q_rows[lax.rem(placement[i], requests)].astype(jnp.bfloat16)
    pl.semaphore_wait(barrier, n_replica + n_tp - 2)

    pending = []

    def send(source, land, slot, peers, send_sem, recv_sem):
        for d, i, device in peers:
            copy = pltpu.make_async_remote_copy(
                src_ref=source(i), dst_ref=land.at[slot],
                send_sem=send_sem.at[d], recv_sem=recv_sem.at[slot],
                device_id=device, device_id_type=MESH,
            )
            copy.start()
            pending.append(copy)

    def deliver(source, land, peer, part):
        d, i, device = peer
        copy = pltpu.make_async_remote_copy(
            src_ref=source, dst_ref=land.at[t],
            send_sem=t_send.at[part, d], recv_sem=t_recv.at[part, t],
            device_id=device, device_id_type=MESH,
        )
        copy.start()
        pending.append(copy)

    def receive(land, peers, send_sem, recv_sem):
        for d, i, device in peers:
            pltpu.make_async_remote_copy(
                src_ref=land.at[i], dst_ref=land.at[i],
                send_sem=send_sem.at[d], recv_sem=recv_sem.at[i],
                device_id=device, device_id_type=MESH,
            ).wait_recv()

    send(lambda i: chosen.at[i], q_land, replica, replicas, a_send, a_recv)
    q_land[replica] = chosen[replica]

    def cache_request(k):
        blocks = [
            cache_v[table[j, k]]
            for j in range(slots)
        ]
        block = jnp.concatenate(blocks, axis=0)

        def take(which):
            return jnp.concatenate(
                [
                    block[:, (2 * h + which) * HEAD_SIZE:(2 * h + which + 1) * HEAD_SIZE]
                    for h in range(local_heads)
                ],
                axis=1,
            )

        scores = dot(spread(q_rows[k].astype(jnp.bfloat16), local_heads, rows // local_heads), take(0), NT) * scale
        seen = lax.broadcasted_iota(jnp.int32, scores.shape, 1) < lengths[k]
        scores = jnp.where(seen, scores, HIDDEN)
        top = jnp.max(scores, axis=1, keepdims=True)
        probs = jnp.where(seen, jnp.exp(scores - top), 0.0)
        total = jnp.sum(probs, axis=1, keepdims=True)
        summed = dot(probs.astype(jnp.bfloat16), take(1), NN)
        c_out[k] = gather_blocks(summed, local_heads, rows // local_heads)
        c_max[k] = jnp.broadcast_to(top, (rows, HEAD_SIZE))
        c_sum[k] = jnp.broadcast_to(total, (rows, HEAD_SIZE))

    def cache_part(first, last):
        def body(step, carry):
            for u in range(2):
                cache_request(first + 2 * step + u)
            return carry

        lax.fori_loop(0, (last - first) // 2, body, 0)

    for copy in cache_copies:
        copy.wait()
    cache_part(0, 5 * requests // 8)

    receive(q_land, replicas, a_send, a_recv)
    q_all[t] = q_land[lax.div(placement[replica], requests)]
    send(lambda i: q_all.at[t], q_all, t, columns, t_send.at[0], t_recv.at[0])
    cache_part(5 * requests // 8, requests)
    receive(q_all, columns, t_send.at[0], t_recv.at[0])

    def weight(slot, which):
        left = (slot // pair_slots) * (4 * HEAD_SIZE) + which * HEAD_SIZE
        return jnp.concatenate(
            [
                w_v[:, pl.ds(pl.multiple_of(left + h * 2 * HEAD_SIZE, HEAD_SIZE), HEAD_SIZE)]
                for h in range(2)
            ],
            axis=1,
        )

    def inside(slot):
        return lax.rem(slot, pair_slots) * rows

    def doubled(value):
        return jnp.concatenate(split(value), axis=0)

    def part_scores(slot):
        q = spread(q_all[slot], 2, pair_rows // 2, inside(slot))
        both = dot(doubled(dot(q, weight(slot, 0), NT)), x_v[...], NT)
        s_part[slot] = both[:rows] + both[rows:]

    def part_sums(slot):
        both = dot(doubled(dot(p_all[slot], x_v[...], NN)), weight(slot, 1), NN)
        o_part[slot] = gather_blocks(both[:rows] + both[rows:], 2, pair_rows // 2, inside(slot))

    for copy in w_copies:
        copy.wait()
    x_copy.wait()
    for peer in columns:
        part_scores(peer[1])
        deliver(s_part.at[peer[1]], s_land, peer, 1)
    part_scores(t)
    receive(s_land, columns, t_send.at[1], t_recv.at[1])

    scores = s_part[t]
    for _, i, _ in columns:
        scores = scores + s_land[i]
    scores = scores * scale
    top = jnp.max(scores, axis=1, keepdims=True)
    probs = jnp.exp(scores - top)
    p_all[t] = probs.astype(jnp.bfloat16)
    send(lambda i: p_all.at[t], p_all, t, columns, t_send.at[2], t_recv.at[2])
    marks[replica, 0] = jnp.broadcast_to(top, (rows, HEAD_SIZE))
    marks[replica, 1] = jnp.broadcast_to(jnp.sum(probs, axis=1, keepdims=True), (rows, HEAD_SIZE))
    send(lambda i: marks.at[replica], marks, replica, replicas, m_send, m_recv)

    part_sums(t)
    for peer in reversed(columns):
        receive(p_all, [peer], t_send.at[2], t_recv.at[2])
        part_sums(peer[1])
        deliver(o_part.at[peer[1]], o_land, peer, 3)

    receive(marks, replicas, m_send, m_recv)

    def prepare(k, carry):
        request = jnp.full((rows, HEAD_SIZE), replica * requests + k, jnp.int32)
        hits = [request == placement[i] for i in range(n_replica)]
        top = c_max[k]
        for i in range(n_replica):
            top = jnp.maximum(top, jnp.where(hits[i], marks[i, 0], HIDDEN))
        kept = jnp.exp(c_max[k] - top)
        total = c_sum[k] * kept
        added = []
        for i in range(n_replica):
            added.append(jnp.where(hits[i], jnp.exp(marks[i, 0] - top), 0.0))
            total = total + marks[i, 1] * added[i]
        inverse = 1.0 / total
        c_out[k] = c_out[k] * (kept * inverse)
        for i in range(n_replica):
            factors[k, i] = added[i] * inverse
        return carry

    lax.fori_loop(0, requests, prepare, 0)
    receive(o_land, columns, t_send.at[3], t_recv.at[3])
    summed = o_part[t]
    for _, i, _ in columns:
        summed = summed + o_land[i]
    state[replica] = summed

    send(lambda i: state.at[replica], state, replica, replicas, e_send, e_recv)
    receive(state, replicas, e_send, e_recv)

    def combine(k, carry):
        summed = c_out[k]
        for i in range(n_replica):
            summed = summed + state[i] * factors[k, i]
        c_out[k] = summed
        return carry

    lax.fori_loop(0, requests, combine, 0)
    for h in range(heads):
        out_ref[:, h * HEAD_SIZE:(h + 1) * HEAD_SIZE] = c_out[:, h, :].astype(out_ref.dtype)
    for copy in pending:
        copy.wait_send()


def local(sizes, span_hidden, key_value_weight, queries, kv_cache, block_table, lengths, placement):
    n_role, n_rep, n_tp = sizes
    n_replica = n_role * n_rep
    requests = queries.shape[0]
    heads = queries.shape[1] // HEAD_SIZE
    rows = max(heads, 16)
    tokens, features = span_hidden.shape
    pool = kv_cache.reshape(-1, PAGE_TOKENS, kv_cache.shape[1])
    bf16, f32 = jnp.bfloat16, jnp.float32
    smem = pl.BlockSpec(memory_space=pltpu.SMEM)
    vmem = pl.BlockSpec(memory_space=pltpu.VMEM)
    hbm = pl.BlockSpec(memory_space=pl.ANY)
    dma = pltpu.SemaphoreType.DMA
    return pl.pallas_call(
        functools.partial(kernel, sizes),
        out_shape=jax.ShapeDtypeStruct(queries.shape, bf16),
        in_specs=[smem, smem, smem, vmem, hbm, hbm, hbm],
        out_specs=vmem,
        scratch_shapes=[
            pltpu.VMEM(span_hidden.shape, bf16),
            pltpu.VMEM(key_value_weight.shape, bf16),
            pltpu.VMEM(pool.shape, bf16),
            pltpu.VMEM((requests, rows, HEAD_SIZE), f32),
            pltpu.VMEM((n_replica, rows, HEAD_SIZE), bf16),
            pltpu.VMEM((n_replica, rows, HEAD_SIZE), bf16),
            pltpu.VMEM((n_tp, rows, HEAD_SIZE), bf16),
            pltpu.VMEM((n_tp, rows, tokens), f32),
            pltpu.VMEM((n_tp, rows, tokens), f32),
            pltpu.VMEM((n_tp, rows, tokens), bf16),
            pltpu.VMEM((n_tp, rows, HEAD_SIZE), f32),
            pltpu.VMEM((n_tp, rows, HEAD_SIZE), f32),
            pltpu.VMEM((n_replica, rows, HEAD_SIZE), f32),
            pltpu.VMEM((n_replica, 2, rows, HEAD_SIZE), f32),
            pltpu.VMEM((requests, n_replica, rows, HEAD_SIZE), f32),
            pltpu.VMEM((requests, rows, HEAD_SIZE), f32),
            pltpu.VMEM((requests, rows, HEAD_SIZE), f32),
            pltpu.VMEM((requests, rows, HEAD_SIZE), f32),
            dma((3 + CHUNKS,)),
            dma((n_replica,)),
            dma((n_replica,)),
            dma((4, n_tp)),
            dma((4, n_tp)),
            dma((n_replica,)),
            dma((n_replica,)),
            dma((n_replica,)),
            dma((n_replica,)),
        ],
        compiler_params=pltpu.CompilerParams(
            collective_id=0, has_side_effects=True, vmem_limit_bytes=60 * 1024 * 1024
        ),
    )(placement, block_table.T, lengths, queries, span_hidden, key_value_weight, pool)


def solution(mesh):
    placed = (
        P(("role", "rep"), "tp"),
        P("tp", None),
        P(("role", "rep"), "tp"),
        P(("role", "rep"), "tp"),
        P(("role", "rep"), None),
        P(("role", "rep")),
        P(),
    )
    sizes = (mesh.shape["role"], mesh.shape["rep"], mesh.shape["tp"])
    return jax.shard_map(
        functools.partial(local, sizes),
        mesh=mesh, in_specs=placed, out_specs=P(("role", "rep"), "tp"), check_vma=False,
    )
```

time: 35.9 us -> 35.9 us (level)
  no operation moved by 1% of the time
where the time goes in v3:
time: 35.9 us; the launch traced here: 35.7 us
  Pallas kernels  34.2 us (95%)
  local copies, waits for them, and re-layouts  1.47 us (4%)
    pallas_call x1, Pallas kernels, local(): pl.pallas_call(functools.partial(kernel, sizes), out_shape=jax.ShapeDtype...  34.2 us
    unnamed x1, local copies, waits for them, and re-layouts  1.47 us

profile of v3, /device:TPU:0, one launch (start us, length us, event | category | flops | bytes accessed | tf_op | source)
XLA Modules:
  0.0 35.7 jit_solution(14224655214492915398)
XLA Ops:
  0.0 34.2 %shard_map.73 = bf16[16,2048]{1,0:T(8,128)(2,1)} custom-call(s32[8]{0:T(128)} %placement.1, s32[4,16]{1,0:T(4,128)} %bitcast.3, s32[16]{0:T(128)} %lengths.1, bf16[16,2048]{1,0:T(8,128)(2,1)} %q_ref.1, bf16[512,2048]{1,0:T(8,128)(2,1)} %x_hbm.1, bf16[2048,2048]{1,0:T(8,128)(2,1)} %w_hbm.1, bf16[36,128,512]{2,1,0:T(8,128)(2,1)} %bitcast.2), custom_call_target="tpu_custom_call" | custom-call | tf_op jit(solution)/shard_map/pallas_call | solution.py:304
  34.2 1.5 %copy.9 = bf16[16,2048]{1,0:T(8,128)(2,1)} copy(bf16[16,2048]{1,0:T(8,128)(2,1)} %shard_map.73) | data formatting | bytes 131072

commit v4 on v3

--- a/solution.py
+++ b/solution.py
@@ -49,7 +49,7 @@
     sizes,
     placement, table, lengths, q_ref, x_hbm, w_hbm, cache_hbm,
     out_ref,
-    x_v, w_v, cache_v, q_rows, chosen, q_land, q_all, s_part, s_land, p_all, o_part, o_land,
+    x_v, w_v, cache_v, q_rows, chosen, q_land, q_all, s_part, s_land, p_all, p_hi, p_lo, o_part, o_land,
     state, marks, factors, c_out, c_max, c_sum,
     local_sem, a_send, a_recv, t_send, t_recv, m_send, m_recv, e_send, e_recv,
 ):
@@ -184,12 +184,12 @@
 
     for copy in cache_copies:
         copy.wait()
-    cache_part(0, 5 * requests // 8)
+    cache_part(0, requests // 2)
 
     receive(q_land, replicas, a_send, a_recv)
     q_all[t] = q_land[lax.div(placement[replica], requests)]
     send(lambda i: q_all.at[t], q_all, t, columns, t_send.at[0], t_recv.at[0])
-    cache_part(5 * requests // 8, requests)
+    cache_part(requests // 2, 3 * requests // 4)
     receive(q_all, columns, t_send.at[0], t_recv.at[0])
 
     def weight(slot, which):
@@ -224,6 +224,7 @@
         part_scores(peer[1])
         deliver(s_part.at[peer[1]], s_land, peer, 1)
     part_scores(t)
+    cache_part(3 * requests // 4, requests)
     receive(s_land, columns, t_send.at[1], t_recv.at[1])
 
     scores = s_part[t]
@@ -238,11 +239,19 @@
     marks[replica, 1] = jnp.broadcast_to(jnp.sum(probs, axis=1, keepdims=True), (rows, HEAD_SIZE))
     send(lambda i: marks.at[replica], marks, replica, replicas, m_send, m_recv)
 
-    part_sums(t)
-    for peer in reversed(columns):
-        receive(p_all, [peer], t_send.at[2], t_recv.at[2])
-        part_sums(peer[1])
-        deliver(o_part.at[peer[1]], o_land, peer, 3)
+    receive(p_all, columns, t_send.at[2], t_recv.at[2])
+    both = dot(p_all[...].reshape(n_tp * rows, p_all.shape[2]), x_v[...], NN)
+    high, low = split(both)
+    wide_hi = high.reshape(n_tp, rows, features)
+    wide_lo = low.reshape(n_tp, rows, features)
+    p_hi[...] = wide_hi
+    p_lo[...] = wide_lo
+    for peer in columns + [(0, t, None)]:
+        slot = peer[1]
+        both = dot(jnp.concatenate([p_hi[slot], p_lo[slot]], axis=0), weight(slot, 1), NN)
+        o_part[slot] = gather_blocks(both[:rows] + both[rows:], 2, pair_rows // 2, inside(slot))
+        if peer[2] is not None:
+            deliver(o_part.at[slot], o_land, peer, 3)
 
     receive(marks, replicas, m_send, m_recv)
 
@@ -264,7 +273,7 @@
             factors[k, i] = added[i] * inverse
         return carry
 
-    lax.fori_loop(0, requests, prepare, 0)
+    lax.fori_loop(0, requests // 2, prepare, 0)
     receive(o_land, columns, t_send.at[3], t_recv.at[3])
     summed = o_part[t]
     for _, i, _ in columns:
@@ -272,6 +281,7 @@
     state[replica] = summed
 
     send(lambda i: state.at[replica], state, replica, replicas, e_send, e_recv)
+    lax.fori_loop(requests // 2, requests, prepare, 0)
     receive(state, replicas, e_send, e_recv)
 
     def combine(k, carry):
@@ -317,6 +327,8 @@
             pltpu.VMEM((n_tp, rows, tokens), f32),
             pltpu.VMEM((n_tp, rows, tokens), f32),
             pltpu.VMEM((n_tp, rows, tokens), bf16),
+            pltpu.VMEM((n_tp, rows, features), bf16),
+            pltpu.VMEM((n_tp, rows, features), bf16),
             pltpu.VMEM((n_tp, rows, HEAD_SIZE), f32),
             pltpu.VMEM((n_tp, rows, HEAD_SIZE), f32),
             pltpu.VMEM((n_replica, rows, HEAD_SIZE), f32),

time: 35.9 us -> 34.3 us (0.955)
  Pallas kernels: 34.2 us -> 32.7 us
    pallas_call x1, Pallas kernels: 34.2 us -> 32.7 us  [local(): pl.pallas_call(functools.partial(kernel, sizes), out_shape=jax.ShapeDtype...]
where the time goes in v4:
time: 34.3 us; the launch traced here: 34.2 us
  Pallas kernels  32.7 us (95%)
  local copies, waits for them, and re-layouts  1.47 us (4%)
    pallas_call x1, Pallas kernels, local(): pl.pallas_call(functools.partial(kernel, sizes), out_shape=jax.ShapeDtype...  32.7 us
    unnamed x1, local copies, waits for them, and re-layouts  1.47 us

profile of v4, /device:TPU:0, one launch (start us, length us, event | category | flops | bytes accessed | tf_op | source)
XLA Modules:
  0.0 34.2 jit_solution(4478087421846757961)
XLA Ops:
  0.0 32.7 %shard_map.73 = bf16[16,2048]{1,0:T(8,128)(2,1)} custom-call(s32[8]{0:T(128)} %placement.1, s32[4,16]{1,0:T(4,128)} %bitcast.3, s32[16]{0:T(128)} %lengths.1, bf16[16,2048]{1,0:T(8,128)(2,1)} %q_ref.1, bf16[512,2048]{1,0:T(8,128)(2,1)} %x_hbm.1, bf16[2048,2048]{1,0:T(8,128)(2,1)} %w_hbm.1, bf16[36,128,512]{2,1,0:T(8,128)(2,1)} %bitcast.2), custom_call_target="tpu_custom_call" | custom-call | tf_op jit(solution)/shard_map/pallas_call | solution.py:314
  32.7 1.5 %copy.9 = bf16[16,2048]{1,0:T(8,128)(2,1)} copy(bf16[16,2048]{1,0:T(8,128)(2,1)} %shard_map.73) | data formatting | bytes 131072
